TPU v7x, 512 devices: a whole 4x4x16 slice. The times are simulated.
512 devices in a mesh: fsdp: 64 (over y, z_hi, x, core), basis: 8 (over z_lo).
Axes of the slice: x: 4, y: 4, z: 16 (z_hi: 2, z_lo: 8; z = z_hi * 8 + z_lo), core: 2. Of those that a mesh axis runs over, the one named last changes fastest.
Arguments:
- activations: bfloat16 [2048, 6144], P('basis', 'fsdp'), may hold values from -6 to 6
- hidden_grad: bfloat16 [2048, 8192], P('basis', 'fsdp'), may hold values from -0.1796875 to 0.1796875
- block_rows: int32 [16], P('basis'), may hold values from 1 to 128, 1280 in all
- basis: bfloat16 [6144, 4096], P('fsdp', 'basis'), may hold values from -0.21875 to 0.21875
- accumulated: float32 [6144, 8192], P('basis', 'fsdp'), may hold values from -3 to 3
Outputs:
- projected: float32 [6144, 8192], P('basis', 'fsdp')
Inputs may be any that keep to these rules, and one draw needn't show every extreme that they name: `block_rows`: every block holds at least one routed token, and some block is full.
All inputs are finite; a program needn't handle non-finite values.
Results may differ from a plain program's by a relative error of at most 0.029.
Values may be sent and summed in bfloat16 or wider, within the bound.
No kernel may reach another device: no remote copies, remote signals or barrier semaphores. Data moves between devices by JAX's collectives and lax.ppermute only.
A program may use at most 64 MiB of HBM per device.

v0:
```python
import jax
import jax.numpy as jnp
from jax import lax
from jax.sharding import PartitionSpec as P

BLOCK = 128


def on_device(activations, hidden_grad, block_rows, basis, accumulated):
    block_size = BLOCK
    tok_count = activations.shape[0]
    blocks_here = block_rows.shape[0]
    position = jnp.arange(tok_count, dtype=jnp.int32)
    block_index = position // block_size
    fill_count = jnp.sum(
        jnp.where(
            block_index[:, None] == jnp.arange(blocks_here, dtype=jnp.int32)[None, :],
            block_rows[None, :],
            0,
        ),
        axis=1,
    )
    live_rows = position % block_size < fill_count
    masked = jnp.where(live_rows[:, None], hidden_grad, jnp.zeros_like(hidden_grad))
    features = lax.all_gather(activations, "fsdp", axis=1, tiled=True)
    partial_value = lax.dot_general(
        features, masked, (((0,), (0,)), ((), ())), preferred_element_type=jnp.float32
    )
    row_count = partial_value.shape[0] // lax.axis_size("basis")
    row_start = lax.axis_index("basis") * row_count
    current = lax.dynamic_slice_in_dim(partial_value, row_start, row_count, 0)
    partial_value = lax.dynamic_update_slice_in_dim(
        partial_value, current + accumulated, row_start, 0
    )
    gradient = lax.psum(partial_value.astype(jnp.bfloat16), "basis")
    own_rows = lax.dynamic_slice_in_dim(gradient, row_start, row_count, 0)
    panel_full = lax.all_gather(basis, "fsdp", axis=0, tiled=True)
    coeff_sum = lax.dot_general(
        panel_full, gradient, (((0,), (0,)), ((), ())), preferred_element_type=jnp.float32
    )
    coeffs = coeff_sum.astype(jnp.bfloat16)
    removal_part = jnp.dot(panel_full, coeffs, preferred_element_type=jnp.float32)
    removed = lax.psum_scatter(
        removal_part.astype(jnp.bfloat16), "basis", scatter_dimension=0, tiled=True
    ).astype(jnp.float32)
    return own_rows.astype(jnp.float32) - removed


def solution(mesh):
    placed = (
        P("basis", "fsdp"),
        P("basis", "fsdp"),
        P("basis"),
        P("fsdp", "basis"),
        P("basis", "fsdp"),
    )
    return jax.shard_map(
        on_device, mesh=mesh, in_specs=placed, out_specs=P("basis", "fsdp"), check_vma=False
    )
```

profile of v0, /device:TPU:12, one launch (start us, length us, event | category | flops | bytes accessed | tf_op | source)
XLA Modules:
  0.0 496.8 jit_solution(16144019380713073946)
XLA Ops:
  6.5 0.0 all-gather.3.cloned.1.call-start
  6.5 0.7 all-gather.3.cloned.1.call-update
  7.3 0.0 all-reduce.2.cloned.1.call-start
  7.3 1.2 copy.8
  8.5 0.7 fusion.6
  9.2 127.1 %all-gather.3.cloned.1.call-done = bf16[256,6144]{0,1:T(8,128)(2,1)} async-done(((bf16[256,96]{0,1:T(8,128)(2,1)}), bf16[256,6144]{0,1:T(8,128)(2,1)}) %all-gather.3.cloned.1.call-update) | async-done | bytes 3145744 | tf_op jit(solution)/shard_map/all_gather | solution.py:25
  136.4 3.2 fusion.2
  139.6 0.3 copy.10
  139.9 0.1 fusion.1
  139.9 1.4 convert_element_type.19
  141.3 0.0 all-reduce.2.cloned.1.call-update
  141.4 0.0 all-gather.5.cloned.1.call-start
  141.4 0.7 all-gather.5.cloned.1.call-update
  142.1 0.0 reduce-scatter.2.cloned.1.call-start
  142.1 124.4 %all-reduce.2.cloned.1.call-done = bf16[6144,128]{0,1:T(8,128)(2,1)} async-done(((bf16[6144,128]{0,1:T(8,128)(2,1)}), bf16[6144,128]{0,1:T(8,128)(2,1)}) %all-reduce.2.cloned.1.call-update) | async-done | bytes 1572880 | tf_op jit(solution)/shard_map/psum | solution.py:35
  266.5 146.4 %all-gather.5.cloned.1.call-done = bf16[6144,512]{1,0:T(8,128)(2,1)} async-done(((bf16[96,512]{1,0:T(8,128)(2,1)}), bf16[6144,512]{1,0:T(8,128)(2,1)}) %all-gather.5.cloned.1.call-update) | async-done | bytes 6291472 | tf_op jit(solution)/shard_map/all_gather | solution.py:37
  412.9 9.3 %fusion = bf16[6144,128]{0,1:T(8,128)(2,1)} fusion(bf16[6144,512]{1,0:T(8,128)(2,1)} %all-gather.5.cloned.1.call-done, bf16[6144,128]{0,1:T(8,128)(2,1)} %all-reduce.2.cloned.1.call-done), kind=kOutput, calls=%fused_computation.1 | convolution fusion | flops 1611464704 | bytes 9437184 | tf_op jit(solution)/shard_map/dot_general | solution.py:42
  422.3 0.0 reduce-scatter.2.cloned.1.call-update
  422.3 66.0 %reduce-scatter.2.cloned.1.call-done = bf16[768,128]{0,1:T(8,128)(2,1)} async-done(((bf16[6144,128]{0,1:T(8,128)(2,1)}), bf16[768,128]{0,1:T(8,128)(2,1)}) %reduce-scatter.2.cloned.1.call-update) | async-done | bytes 196624 | tf_op jit(solution)/shard_map/reduce_scatter | solution.py:43
  488.3 1.1 convert_subtract_fusion
  489.3 0.9 copy.9
  (2 shorter events, 0.0 us)
Async XLA Ops:
  6.5 129.8 %all-gather.3.cloned.1.call-start = ((), (), s32[]{:S(2)}) async-start(), calls=%async_computation.1 | async-start | bytes 3194880 | tf_op jit(solution)/shard_map/all_gather | solution.py:25
  7.3 259.3 %all-reduce.2.cloned.1.call-start = ((), (), s32[]{:S(2)}) async-start(), calls=%async_computation.2 | async-start | bytes 3145728 | tf_op jit(solution)/shard_map/psum | solution.py:35
  141.4 271.6 %all-gather.5.cloned.1.call-start = ((), (), s32[]{:S(2)}) async-start(), calls=%async_computation.3 | async-start | bytes 6389760 | tf_op jit(solution)/shard_map/all_gather | solution.py:37
  142.1 346.2 %reduce-scatter.2.cloned.1.call-start = ((), (), s32[]{:S(2)}) async-start(), calls=%async_computation.4 | async-start | bytes 1769472 | tf_op jit(solution)/shard_map/reduce_scatter | solution.py:43
Sparse Core Ops, SparseCore 0:
  11.9 124.4 all-gather.2
  141.5 124.9 all-reduce.1
  271.0 141.8 all-gather.4
  422.4 65.8 reduce-scatter.1
where the time goes:
time: 497 us
  waiting for transfers between devices  465 us (94%)
  between operations  13.2 us (3%)
  matrix products  12.5 us (3%)
    all_gather x1, waiting for transfers between devices, on_device(): panel_full = lax.all_gather(basis, 'fsdp', axis=0, tiled=True)  146 us
    all_gather x1, waiting for transfers between devices, on_device(): features = lax.all_gather(activations, 'fsdp', axis=1, tiled=True)  127 us
    psum x1, waiting for transfers between devices, on_device(): gradient = lax.psum(partial_value.astype(jnp.bfloat16), 'basis')  124 us
    reduce_scatter x1, waiting for transfers between devices, on_device(): lax.psum_scatter(removal_part.astype(jnp.bfloat16), 'basis', scatter_dime...  66 us
  transfers between devices with their start and end apart: 4, of which 4 were waited for; matrix products, arithmetic and copies ran while one was open for 0% of the time, Pallas kernels for 0%

commit v1 on v0

--- a/solution.py
+++ b/solution.py
@@ -34,7 +34,15 @@
     )
     gradient = lax.psum(partial_value.astype(jnp.bfloat16), "basis")
     own_rows = lax.dynamic_slice_in_dim(gradient, row_start, row_count, 0)
-    panel_full = lax.all_gather(basis, "fsdp", axis=0, tiled=True)
+    panel_full = jnp.concatenate(
+        lax.all_to_all(
+            jnp.stack([basis] * lax.psum(1, axis_name="fsdp"), 0),
+            axis_name="fsdp",
+            split_axis=0,
+            concat_axis=0,
+        ),
+        0,
+    )
     coeff_sum = lax.dot_general(
         panel_full, gradient, (((0,), (0,)), ((), ())), preferred_element_type=jnp.float32
     )

time: 497 us -> 597 us (1.20)
  the two profiles are of different devices: /device:TPU:12 before, /device:TPU:4 now
where the time goes in v1:
time: 597 us
  waiting for transfers between devices  542 us (91%)
  starting transfers between devices  21.7 us (4%)
  between operations  13.2 us (2%)
  matrix products  12.4 us (2%)
    all_gather x1, waiting for transfers between devices, on_device(): features = lax.all_gather(activations, 'fsdp', axis=1, tiled=True)  351 us
    psum x1, waiting for transfers between devices, on_device(): gradient = lax.psum(partial_value.astype(jnp.bfloat16), 'basis')  124 us
    reduce_scatter x1, waiting for transfers between devices, on_device(): lax.psum_scatter(removal_part.astype(jnp.bfloat16), 'basis', scatter_dime...  65.9 us
    all_to_all x1, starting transfers between devices, on_device(): lax.all_to_all(jnp.stack([basis] * lax.psum(1, axis_name='fsdp'), 0), axi...  21.5 us
  transfers between devices with their start and end apart: 4, of which 3 were waited for; matrix products, arithmetic and copies ran while one was open for 1% of the time, Pallas kernels for 0%

profile of v1, /device:TPU:4, one launch (start us, length us, event | category | flops | bytes accessed | tf_op | source)
XLA Modules:
  0.0 597.2 jit_solution(13193170596614928737)
XLA Ops:
  6.5 4.3 stack.2
  10.8 0.0 copy-start
  10.8 0.0 copy-start.2
  10.8 0.0 copy-start.1
  10.8 21.5 %all-to-all-start = ((bf16[64,96,512]{2,1,0:T(8,128)(2,1)}), bf16[64,96,512]{2,1,0:T(8,128)(2,1)}, u32[]{:S(2)}, u32[]{:S(2)}) async-start(bf16[64,96,512]{2,1,0:T(8,128)(2,1)} %stack.2), calls=%async_computation | async-start | bytes 12582912 | tf_op jit(solution)/shard_map/all_to_all | solution.py:38
  32.4 0.0 all-gather.2.cloned.1.call-start
  32.4 0.7 all-gather.2.cloned.1.call-update
  33.1 0.0 all-reduce.2.cloned.1.call-start
  33.2 0.0 copy-done
  33.2 0.2 copy.8
  33.4 0.0 copy-done.2
  33.4 0.1 fusion.6
  33.5 350.9 %all-gather.2.cloned.1.call-done = bf16[256,6144]{0,1:T(8,128)(2,1)} async-done(((bf16[256,96]{0,1:T(8,128)(2,1)}), bf16[256,6144]{0,1:T(8,128)(2,1)}) %all-gather.2.cloned.1.call-update) | async-done | bytes 3145744 | tf_op jit(solution)/shard_map/all_gather | solution.py:25
  384.4 0.0 copy-done.1
  384.4 3.1 fusion.2
  387.5 0.3 copy.10
  387.8 0.1 fusion.1
  387.9 1.3 convert_element_type.19
  389.2 0.0 all-reduce.2.cloned.1.call-update
  389.2 0.0 reduce-scatter.2.cloned.1.call-start
  389.3 124.2 %all-reduce.2.cloned.1.call-done = bf16[6144,128]{0,1:T(8,128)(2,1)} async-done(((bf16[6144,128]{0,1:T(8,128)(2,1)}), bf16[6144,128]{0,1:T(8,128)(2,1)}) %all-reduce.2.cloned.1.call-update) | async-done | bytes 1572880 | tf_op jit(solution)/shard_map/psum | solution.py:35
  513.5 0.0 all-to-all-done
  513.5 9.3 %fusion = bf16[6144,128]{0,1:T(8,128)(2,1)} fusion(bf16[6144,512]{1,0:T(8,128)(2,1)} %bitcast.2, bf16[6144,128]{0,1:T(8,128)(2,1)} %all-reduce.2.cloned.1.call-done), kind=kOutput, calls=%fused_computation.1 | convolution fusion | flops 1611464704 | bytes 9437184 | tf_op jit(solution)/shard_map/dot_general | solution.py:50
  522.7 0.0 reduce-scatter.2.cloned.1.call-update
  522.8 65.9 %reduce-scatter.2.cloned.1.call-done = bf16[768,128]{0,1:T(8,128)(2,1)} async-done(((bf16[6144,128]{0,1:T(8,128)(2,1)}), bf16[768,128]{0,1:T(8,128)(2,1)}) %reduce-scatter.2.cloned.1.call-update) | async-done | bytes 196624 | tf_op jit(solution)/shard_map/reduce_scatter | solution.py:51
  588.7 1.1 convert_subtract_fusion
  589.7 0.9 copy.9
  (2 shorter events, 0.0 us)
Async XLA Ops:
  10.8 22.3 %copy-start = (f32[768,128]{1,0:T(8,128)S(1)}, f32[768,128]{1,0:T(8,128)}, u32[]{:S(2)}) copy-start(f32[768,128]{1,0:T(8,128)} %param.9) | copy-start | bytes 1179652
  10.8 22.5 %copy-start.2 = (s32[2]{0:T(128)S(1)}, s32[2]{0:T(128)}, u32[]{:S(2)}) copy-start(s32[2]{0:T(128)} %param.7) | copy-start | bytes 28
  10.8 373.5 %copy-start.1 = (bf16[256,128]{1,0:T(8,128)(2,1)S(1)}, bf16[256,128]{1,0:T(8,128)(2,1)}, u32[]{:S(2)}) copy-start(bf16[256,128]{1,0:T(8,128)(2,1)} %param.6) | copy-start | bytes 196612
  10.8 502.6 %all-to-all-start = ((bf16[64,96,512]{2,1,0:T(8,128)(2,1)}), bf16[64,96,512]{2,1,0:T(8,128)(2,1)}, u32[]{:S(2)}, u32[]{:S(2)}) async-start(bf16[64,96,512]{2,1,0:T(8,128)(2,1)} %stack.2), calls=%async_computation | async-start | bytes 12582912 | tf_op jit(solution)/shard_map/all_to_all | solution.py:38
  32.4 352.0 %all-gather.2.cloned.1.call-start = ((), (), s32[]{:S(2)}) async-start(), calls=%async_computation.2 | async-start | bytes 3194880 | tf_op jit(solution)/shard_map/all_gather | solution.py:25
  33.1 480.4 %all-reduce.2.cloned.1.call-start = ((), (), s32[]{:S(2)}) async-start(), calls=%async_computation.3 | async-start | bytes 3145728 | tf_op jit(solution)/shard_map/psum | solution.py:35
  389.2 199.4 %reduce-scatter.2.cloned.1.call-start = ((), (), s32[]{:S(2)}) async-start(), calls=%async_computation.4 | async-start | bytes 1769472 | tf_op jit(solution)/shard_map/reduce_scatter | solution.py:51
Sparse Core Ops, SparseCore 0:
  37.7 346.5 all-gather.1
  389.4 124.0 all-reduce.1
  522.9 65.7 reduce-scatter.1

commit v2 on v0

--- a/solution.py
+++ b/solution.py
@@ -32,7 +32,9 @@
     partial_value = lax.dynamic_update_slice_in_dim(
         partial_value, current + accumulated, row_start, 0
     )
-    gradient = lax.psum(partial_value.astype(jnp.bfloat16), "basis")
+    x = partial_value.astype(jnp.bfloat16)
+    parts = lax.all_gather(x, "basis", axis=0, tiled=False)
+    gradient = parts.sum(axis=0)
     own_rows = lax.dynamic_slice_in_dim(gradient, row_start, row_count, 0)
     panel_full = lax.all_gather(basis, "fsdp", axis=0, tiled=True)
     coeff_sum = lax.dot_general(

time: 497 us -> 624 us (1.26)
  the two profiles are of different devices: /device:TPU:12 before, /device:TPU:4 now
where the time goes in v2:
time: 624 us
  waiting for transfers between devices  572 us (92%)
  local copies, waits for them, and re-layouts  14.1 us (2%)
  between operations  13.2 us (2%)
  other arithmetic  12.2 us (2%)
  matrix products  12.1 us (2%)
    all_gather x1, waiting for transfers between devices, on_device(): parts = lax.all_gather(x, 'basis', axis=0, tiled=False)  249 us
    all_gather x1, waiting for transfers between devices, on_device(): panel_full = lax.all_gather(basis, 'fsdp', axis=0, tiled=True)  130 us
    all_gather x1, waiting for transfers between devices, on_device(): features = lax.all_gather(activations, 'fsdp', axis=1, tiled=True)  128 us
    reduce_scatter x1, waiting for transfers between devices, on_device(): lax.psum_scatter(removal_part.astype(jnp.bfloat16), 'basis', scatter_dime...  63.9 us
    unnamed x3, local copies, waits for them, and re-layouts  13.2 us
  transfers between devices with their start and end apart: 4, of which 4 were waited for; matrix products, arithmetic and copies ran while one was open for 4% of the time, Pallas kernels for 0%

profile of v2, /device:TPU:4, one launch (start us, length us, event | category | flops | bytes accessed | tf_op | source)
XLA Modules:
  0.0 623.5 jit_solution(16785186358180661422)
XLA Ops:
  6.5 0.0 all-gather.5.cloned.1.call-start
  6.5 0.7 all-gather.5.cloned.1.call-update
  7.3 0.0 all-gather.9.cloned.1.call-start
  7.3 1.2 copy.8
  8.5 0.7 fusion.6
  9.2 127.9 %all-gather.5.cloned.1.call-done = bf16[256,6144]{0,1:T(8,128)(2,1)} async-done(((bf16[256,96]{0,1:T(8,128)(2,1)}), bf16[256,6144]{0,1:T(8,128)(2,1)}) %all-gather.5.cloned.1.call-update) | async-done | bytes 3145744 | tf_op jit(solution)/shard_map/all_gather | solution.py:25
  137.1 3.2 fusion.2
  140.3 0.3 copy.11
  140.6 0.1 fusion.1
  140.6 1.3 convert_element_type.21
  142.0 0.0 all-gather.9.cloned.1.call-update
  142.0 0.0 all-gather.7.cloned.1.call-start
  142.1 0.7 all-gather.7.cloned.1.call-update
  142.7 0.0 reduce-scatter.2.cloned.1.call-start
  142.8 249.0 %all-gather.9.cloned.1.call-done = bf16[49152,128]{0,1:T(8,128)(2,1)} async-done(((bf16[6144,128]{0,1:T(8,128)(2,1)}), bf16[49152,128]{0,1:T(8,128)(2,1)}) %all-gather.9.cloned.1.call-update) | async-done | bytes 12582928 | tf_op jit(solution)/shard_map/all_gather | solution.py:36
  391.8 11.7 %copy.10 = bf16[16,8,8,6144]{3,2,1,0:T(8,128)(2,1)S(1)} copy(bf16[16,8,8,6144]{3,1,2,0:T(8,128)(2,1)} %bitcast.17) | data formatting | bytes 25165824
  403.6 9.1 %bitcast_reduce_fusion = bf16[6144,128]{0,1:T(8,128)(2,1)S(1)} fusion(bf16[16,8,8,6144]{3,2,1,0:T(8,128)(2,1)S(1)} %copy.10), kind=kLoop, calls=%fused_computation | loop fusion | flops 5505024 | bytes 14155776 | tf_op jit(solution)/shard_map/reduce_sum | solution.py:37
  412.7 129.6 %all-gather.7.cloned.1.call-done = bf16[6144,512]{1,0:T(8,128)(2,1)} async-done(((bf16[96,512]{1,0:T(8,128)(2,1)}), bf16[6144,512]{1,0:T(8,128)(2,1)}) %all-gather.7.cloned.1.call-update) | async-done | bytes 6291472 | tf_op jit(solution)/shard_map/all_gather | solution.py:39
  542.2 8.9 %fusion = bf16[6144,128]{0,1:T(8,128)(2,1)} fusion(bf16[6144,512]{1,0:T(8,128)(2,1)} %all-gather.7.cloned.1.call-done, bf16[6144,128]{0,1:T(8,128)(2,1)S(1)} %bitcast_reduce_fusion), kind=kOutput, calls=%fused_computation.2 | convolution fusion | flops 1611464704 | bytes 9437184 | tf_op jit(solution)/shard_map/dot_general | solution.py:44
  551.1 0.0 reduce-scatter.2.cloned.1.call-update
  551.2 63.9 %reduce-scatter.2.cloned.1.call-done = bf16[768,128]{0,1:T(8,128)(2,1)} async-done(((bf16[6144,128]{0,1:T(8,128)(2,1)}), bf16[768,128]{0,1:T(8,128)(2,1)}) %reduce-scatter.2.cloned.1.call-update) | async-done | bytes 196624 | tf_op jit(solution)/shard_map/reduce_scatter | solution.py:45
  615.1 1.0 convert_subtract_fusion
  616.1 0.9 copy.9
  (2 shorter events, 0.0 us)
Async XLA Ops:
  6.5 130.6 %all-gather.5.cloned.1.call-start = ((), (), s32[]{:S(2)}) async-start(), calls=%async_computation.1 | async-start | bytes 3194880 | tf_op jit(solution)/shard_map/all_gather | solution.py:25
  7.3 384.6 %all-gather.9.cloned.1.call-start = ((), (), s32[]{:S(2)}) async-start(), calls=%async_computation.4 | async-start | bytes 14155776 | tf_op jit(solution)/shard_map/all_gather | solution.py:36
  142.0 400.2 %all-gather.7.cloned.1.call-start = ((), (), s32[]{:S(2)}) async-start(), calls=%async_computation.2 | async-start | bytes 6389760 | tf_op jit(solution)/shard_map/all_gather | solution.py:39
  142.7 472.3 %reduce-scatter.2.cloned.1.call-start = ((), (), s32[]{:S(2)}) async-start(), calls=%async_computation.3 | async-start | bytes 1769472 | tf_op jit(solution)/shard_map/reduce_scatter | solution.py:45
Sparse Core Ops, SparseCore 0:
  11.9 125.1 all-gather.4
  142.1 249.6 all-gather.8
  396.4 145.8 all-gather.6
  551.3 63.7 reduce-scatter.1
